TPU v7x, 1024 devices: a whole 4x4x32 slice. The times are simulated.
1024 devices in a mesh: loss: 64 (over z_lo, x), section: 4 (over y), mp: 4 (over z_hi, core).
Axes of the slice: x: 4, y: 4, z: 32 (z_hi: 2, z_lo: 16; z = z_hi * 16 + z_lo), core: 2. Of those that a mesh axis runs over, the one named last changes fastest.
Arguments:
- image_embed: bfloat16 [16384, 1152], P('loss'), may hold values from -0.1796875 to 0.1796875
- text_embed: bfloat16 [16384, 1152], P(('loss', 'section', 'mp')), may hold values from -0.1796875 to 0.1796875
- logit_scale: float32 [], replicated, may hold values from 4 to 16
- logit_bias: float32 [], replicated, may hold values from -3 to -1
Outputs:
- grad_image: float32 [16384, 1152], P(('loss', 'section', 'mp'))
- grad_text: float32 [16384, 1152], P(('loss', 'section', 'mp'))
All inputs are finite; a program needn't handle non-finite values.
Results may differ from a plain program's by a relative error of at most 0.017.
Values may be sent and summed in bfloat16 or wider, within the bound.
A program may use at most 32 MiB of HBM per device.

v0:
```python
import jax
import jax.numpy as jnp
from jax import lax
from jax.sharding import PartitionSpec as P

epsilon = 1e-06


def shifted(value, axis, steps):
    count = lax.axis_size(axis)
    pairs = [(source, (source + steps) % count) for source in range(count)]
    return lax.ppermute(value, axis, pairs)


def unit_rows(values):
    widened = values.astype(jnp.float32)
    scaling = lax.rsqrt(jnp.sum(widened * widened, axis=-1, keepdims=True) + epsilon)
    return (widened * scaling, scaling)


def unit_backward(unit, scaling, gradient):
    return (gradient - unit * jnp.sum(unit * gradient, axis=-1, keepdims=True)) * scaling


def per_device(image_embed, text_embed, logit_scale, logit_bias):
    unit_image, image_scaling = unit_rows(image_embed)
    unit_text, text_scaling = unit_rows(text_embed)
    image_low = unit_image.astype(jnp.bfloat16)
    text_low = unit_text.astype(jnp.bfloat16)
    image_rows = image_low.shape[0]
    text_rows = text_low.shape[0]
    width = image_low.shape[1]
    cycle_size = lax.axis_size("loss")
    group_index = lax.axis_index("section") * lax.axis_size("mp") + lax.axis_index("mp")
    group_offset = group_index * text_rows
    text_ids = jnp.arange(text_rows, dtype=jnp.int32)[:, None]
    image_cols = jnp.arange(image_rows, dtype=jnp.int32)[None, :] - group_offset
    diagonal = (text_ids == image_cols).astype(jnp.float32)

    def visit(stop_index, carried):
        block, text_grad, dlogit_stash, text_stash = carried
        logits = (
            logit_scale * jnp.dot(block, image_low.T, preferred_element_type=jnp.float32)
            + logit_bias
        )
        positive = jnp.where(stop_index == 0, diagonal, jnp.zeros_like(diagonal))
        dlogit = (jax.nn.sigmoid(logits) - positive).astype(jnp.bfloat16)
        text_grad = text_grad + logit_scale * jnp.dot(
            dlogit, image_low, preferred_element_type=jnp.float32
        )
        dlogit_stash = lax.dynamic_update_slice(dlogit_stash, dlogit[None], (stop_index, 0, 0))
        text_stash = lax.dynamic_update_slice(text_stash, block[None], (stop_index, 0, 0))
        block = shifted(block, "loss", 1)
        text_grad = shifted(text_grad, "loss", 1)
        return (block, text_grad, dlogit_stash, text_stash)

    start = (
        text_low,
        jnp.zeros((text_rows, width), jnp.float32),
        jnp.zeros((cycle_size, text_rows, image_rows), jnp.bfloat16),
        jnp.zeros((cycle_size, text_rows, width), jnp.bfloat16),
    )
    finished = lax.fori_loop(0, cycle_size, visit, start)
    text_grad = finished[1]
    dlogit_all = finished[2].reshape(cycle_size * text_rows, image_rows)
    texts_seen = finished[3].reshape(cycle_size * text_rows, width)
    image_grad = logit_scale * jnp.einsum(
        "ti,te->ie", dlogit_all, texts_seen, preferred_element_type=jnp.float32
    )
    image_share = lax.psum_scatter(
        image_grad.astype(jnp.bfloat16), ("section", "mp"), scatter_dimension=0, tiled=True
    ).astype(jnp.float32)
    own_unit = lax.dynamic_slice_in_dim(unit_image, group_offset, text_rows, 0)
    own_scaling = lax.dynamic_slice_in_dim(image_scaling, group_offset, text_rows, 0)
    grad_image = unit_backward(own_unit, own_scaling, image_share)
    grad_text = unit_backward(unit_text, text_scaling, text_grad)
    return (grad_image, grad_text)


def solution(mesh):
    placed = (P("loss", None), P(("loss", "section", "mp"), None), P(), P())
    return jax.shard_map(
        per_device,
        mesh=mesh,
        in_specs=placed,
        out_specs=(P(("loss", "section", "mp"), None), P(("loss", "section", "mp"), None)),
        check_vma=False,
    )
```

profile of v0, /device:TPU:6, one launch (start us, length us, event | category | flops | bytes accessed | tf_op | source)
XLA Modules:
  0.0 2072.8 jit_solution(4706593237324282190)
XLA Ops:
  13.2 1845.9 %while.20 = (s32[]{:T(128)}, bf16[16,1152]{1,0:T(8,128)(2,1)S(1)}, f32[16,1152]{1,0:T(8,128)S(1)}, bf16[64,16,256]{2,1,0:T(8,128)(2,1)}, bf16[64,16,1152]{2,1,0:...) while((s32[]{:T(128)}, bf16[16,1152]{1,0:T(8,128)(2,1)S(1)}, ...), condition=%wide.region_3.4_spmd.clone, body=%wide.region_2.3_spmd.clone.sunk | while | flops 18952196 | bytes 1981135 | solution.py:63
  121.3 17.3 collective-permute-done
  416.7 17.3 collective-permute-done
  446.5 17.4 collective-permute-done
  476.2 17.3 collective-permute-done
  535.2 17.6 collective-permute-done
  595.0 17.4 collective-permute-done
  654.0 17.4 collective-permute-done
  683.6 17.6 collective-permute-done
  831.2 17.3 collective-permute-done
  919.8 17.3 collective-permute-done
  1097.1 17.3 collective-permute-done
  1186.0 17.3 collective-permute-done
  1215.5 17.3 collective-permute-done
  1274.7 17.6 collective-permute-done
  1334.5 17.3 collective-permute-done
  1393.4 17.4 collective-permute-done
  1422.9 17.6 collective-permute-done
  1452.5 17.3 collective-permute-done
  1570.6 17.3 collective-permute-done
  1600.1 17.3 collective-permute-done
  1659.2 17.3 collective-permute-done
  1718.3 17.3 collective-permute-done
  1862.8 200.5 %reduce-scatter.2.cloned.1.call-done = bf16[16,1152]{1,0:T(8,128)(2,1)} async-done(((bf16[256,1152]{1,0:T(8,128)(2,1)}), bf16[16,1152]{1,0:T(8,128)(2,1)}) %reduce-scatter.2.cloned.1.call-update) | async-done | bytes 36880 | tf_op jit(solution)/shard_map/reduce_scatter | solution.py:70
  (510 shorter events, 1473.6 us)
Async XLA Ops:
  7.2 2056.2 %reduce-scatter.2.cloned.1.call-start = ((), (), s32[]{:S(2)}) async-start(), calls=%async_computation.1 | async-start | bytes 626688 | tf_op jit(solution)/shard_map/reduce_scatter | solution.py:70
  89.8 24.6 %collective-permute-start.1 = (f32[16,1152]{1,0:T(8,128)S(1)}, f32[16,1152]{1,0:T(8,128)S(1)}, u32[]{:S(2)}, u32[]{:S(2)}) collective-permute-start(f32[16,1152]{1,0:T(8,128)S(1)} %fusion.38), channel_id=1, source_target_pairs={{0,16},{16,32},{32,48},{48,64},{64,80},{80,96},{96,112},{112,128},... | collective-permute-start | bytes 221192 | tf_op jit(solution)/shard_map/while/body/eval_jaxpr/ppermute | solution.py:12
  148.9 24.6 %collective-permute-start.1 = (f32[16,1152]{1,0:T(8,128)S(1)}, f32[16,1152]{1,0:T(8,128)S(1)}, u32[]{:S(2)}, u32[]{:S(2)}) collective-permute-start(f32[16,1152]{1,0:T(8,128)S(1)} %fusion.38), channel_id=1, source_target_pairs={{0,16},{16,32},{32,48},{48,64},{64,80},{80,96},{96,112},{112,128},... | collective-permute-start | bytes 221192 | tf_op jit(solution)/shard_map/while/body/eval_jaxpr/ppermute | solution.py:12
  178.4 24.6 %collective-permute-start.1 = (f32[16,1152]{1,0:T(8,128)S(1)}, f32[16,1152]{1,0:T(8,128)S(1)}, u32[]{:S(2)}, u32[]{:S(2)}) collective-permute-start(f32[16,1152]{1,0:T(8,128)S(1)} %fusion.38), channel_id=1, source_target_pairs={{0,16},{16,32},{32,48},{48,64},{64,80},{80,96},{96,112},{112,128},... | collective-permute-start | bytes 221192 | tf_op jit(solution)/shard_map/while/body/eval_jaxpr/ppermute | solution.py:12
  208.0 24.6 %collective-permute-start.1 = (f32[16,1152]{1,0:T(8,128)S(1)}, f32[16,1152]{1,0:T(8,128)S(1)}, u32[]{:S(2)}, u32[]{:S(2)}) collective-permute-start(f32[16,1152]{1,0:T(8,128)S(1)} %fusion.38), channel_id=1, source_target_pairs={{0,16},{16,32},{32,48},{48,64},{64,80},{80,96},{96,112},{112,128},... | collective-permute-start | bytes 221192 | tf_op jit(solution)/shard_map/while/body/eval_jaxpr/ppermute | solution.py:12
  237.5 24.6 %collective-permute-start.1 = (f32[16,1152]{1,0:T(8,128)S(1)}, f32[16,1152]{1,0:T(8,128)S(1)}, u32[]{:S(2)}, u32[]{:S(2)}) collective-permute-start(f32[16,1152]{1,0:T(8,128)S(1)} %fusion.38), channel_id=1, source_target_pairs={{0,16},{16,32},{32,48},{48,64},{64,80},{80,96},{96,112},{112,128},... | collective-permute-start | bytes 221192 | tf_op jit(solution)/shard_map/while/body/eval_jaxpr/ppermute | solution.py:12
  267.0 24.6 %collective-permute-start.1 = (f32[16,1152]{1,0:T(8,128)S(1)}, f32[16,1152]{1,0:T(8,128)S(1)}, u32[]{:S(2)}, u32[]{:S(2)}) collective-permute-start(f32[16,1152]{1,0:T(8,128)S(1)} %fusion.38), channel_id=1, source_target_pairs={{0,16},{16,32},{32,48},{48,64},{64,80},{80,96},{96,112},{112,128},... | collective-permute-start | bytes 221192 | tf_op jit(solution)/shard_map/while/body/eval_jaxpr/ppermute | solution.py:12
  296.6 24.6 %collective-permute-start.1 = (f32[16,1152]{1,0:T(8,128)S(1)}, f32[16,1152]{1,0:T(8,128)S(1)}, u32[]{:S(2)}, u32[]{:S(2)}) collective-permute-start(f32[16,1152]{1,0:T(8,128)S(1)} %fusion.38), channel_id=1, source_target_pairs={{0,16},{16,32},{32,48},{48,64},{64,80},{80,96},{96,112},{112,128},... | collective-permute-start | bytes 221192 | tf_op jit(solution)/shard_map/while/body/eval_jaxpr/ppermute | solution.py:12
  326.1 24.6 %collective-permute-start.1 = (f32[16,1152]{1,0:T(8,128)S(1)}, f32[16,1152]{1,0:T(8,128)S(1)}, u32[]{:S(2)}, u32[]{:S(2)}) collective-permute-start(f32[16,1152]{1,0:T(8,128)S(1)} %fusion.38), channel_id=1, source_target_pairs={{0,16},{16,32},{32,48},{48,64},{64,80},{80,96},{96,112},{112,128},... | collective-permute-start | bytes 221192 | tf_op jit(solution)/shard_map/while/body/eval_jaxpr/ppermute | solution.py:12
  355.7 24.6 %collective-permute-start.1 = (f32[16,1152]{1,0:T(8,128)S(1)}, f32[16,1152]{1,0:T(8,128)S(1)}, u32[]{:S(2)}, u32[]{:S(2)}) collective-permute-start(f32[16,1152]{1,0:T(8,128)S(1)} %fusion.38), channel_id=1, source_target_pairs={{0,16},{16,32},{32,48},{48,64},{64,80},{80,96},{96,112},{112,128},... | collective-permute-start | bytes 221192 | tf_op jit(solution)/shard_map/while/body/eval_jaxpr/ppermute | solution.py:12
  385.2 24.6 %collective-permute-start.1 = (f32[16,1152]{1,0:T(8,128)S(1)}, f32[16,1152]{1,0:T(8,128)S(1)}, u32[]{:S(2)}, u32[]{:S(2)}) collective-permute-start(f32[16,1152]{1,0:T(8,128)S(1)} %fusion.38), channel_id=1, source_target_pairs={{0,16},{16,32},{32,48},{48,64},{64,80},{80,96},{96,112},{112,128},... | collective-permute-start | bytes 221192 | tf_op jit(solution)/shard_map/while/body/eval_jaxpr/ppermute | solution.py:12
  414.7 24.8 %collective-permute-start.1 = (f32[16,1152]{1,0:T(8,128)S(1)}, f32[16,1152]{1,0:T(8,128)S(1)}, u32[]{:S(2)}, u32[]{:S(2)}) collective-permute-start(f32[16,1152]{1,0:T(8,128)S(1)} %fusion.38), channel_id=1, source_target_pairs={{0,16},{16,32},{32,48},{48,64},{64,80},{80,96},{96,112},{112,128},... | collective-permute-start | bytes 221192 | tf_op jit(solution)/shard_map/while/body/eval_jaxpr/ppermute | solution.py:12
  444.5 24.7 %collective-permute-start.1 = (f32[16,1152]{1,0:T(8,128)S(1)}, f32[16,1152]{1,0:T(8,128)S(1)}, u32[]{:S(2)}, u32[]{:S(2)}) collective-permute-start(f32[16,1152]{1,0:T(8,128)S(1)} %fusion.38), channel_id=1, source_target_pairs={{0,16},{16,32},{32,48},{48,64},{64,80},{80,96},{96,112},{112,128},... | collective-permute-start | bytes 221192 | tf_op jit(solution)/shard_map/while/body/eval_jaxpr/ppermute | solution.py:12
  474.2 24.6 %collective-permute-start.1 = (f32[16,1152]{1,0:T(8,128)S(1)}, f32[16,1152]{1,0:T(8,128)S(1)}, u32[]{:S(2)}, u32[]{:S(2)}) collective-permute-start(f32[16,1152]{1,0:T(8,128)S(1)} %fusion.38), channel_id=1, source_target_pairs={{0,16},{16,32},{32,48},{48,64},{64,80},{80,96},{96,112},{112,128},... | collective-permute-start | bytes 221192 | tf_op jit(solution)/shard_map/while/body/eval_jaxpr/ppermute | solution.py:12
  503.7 24.6 %collective-permute-start.1 = (f32[16,1152]{1,0:T(8,128)S(1)}, f32[16,1152]{1,0:T(8,128)S(1)}, u32[]{:S(2)}, u32[]{:S(2)}) collective-permute-start(f32[16,1152]{1,0:T(8,128)S(1)} %fusion.38), channel_id=1, source_target_pairs={{0,16},{16,32},{32,48},{48,64},{64,80},{80,96},{96,112},{112,128},... | collective-permute-start | bytes 221192 | tf_op jit(solution)/shard_map/while/body/eval_jaxpr/ppermute | solution.py:12
  533.3 25.3 %collective-permute-start.1 = (f32[16,1152]{1,0:T(8,128)S(1)}, f32[16,1152]{1,0:T(8,128)S(1)}, u32[]{:S(2)}, u32[]{:S(2)}) collective-permute-start(f32[16,1152]{1,0:T(8,128)S(1)} %fusion.38), channel_id=1, source_target_pairs={{0,16},{16,32},{32,48},{48,64},{64,80},{80,96},{96,112},{112,128},... | collective-permute-start | bytes 221192 | tf_op jit(solution)/shard_map/while/body/eval_jaxpr/ppermute | solution.py:12
  563.5 24.6 %collective-permute-start.1 = (f32[16,1152]{1,0:T(8,128)S(1)}, f32[16,1152]{1,0:T(8,128)S(1)}, u32[]{:S(2)}, u32[]{:S(2)}) collective-permute-start(f32[16,1152]{1,0:T(8,128)S(1)} %fusion.38), channel_id=1, source_target_pairs={{0,16},{16,32},{32,48},{48,64},{64,80},{80,96},{96,112},{112,128},... | collective-permute-start | bytes 221192 | tf_op jit(solution)/shard_map/while/body/eval_jaxpr/ppermute | solution.py:12
  593.1 24.7 %collective-permute-start.1 = (f32[16,1152]{1,0:T(8,128)S(1)}, f32[16,1152]{1,0:T(8,128)S(1)}, u32[]{:S(2)}, u32[]{:S(2)}) collective-permute-start(f32[16,1152]{1,0:T(8,128)S(1)} %fusion.38), channel_id=1, source_target_pairs={{0,16},{16,32},{32,48},{48,64},{64,80},{80,96},{96,112},{112,128},... | collective-permute-start | bytes 221192 | tf_op jit(solution)/shard_map/while/body/eval_jaxpr/ppermute | solution.py:12
  652.1 24.6 %collective-permute-start.1 = (f32[16,1152]{1,0:T(8,128)S(1)}, f32[16,1152]{1,0:T(8,128)S(1)}, u32[]{:S(2)}, u32[]{:S(2)}) collective-permute-start(f32[16,1152]{1,0:T(8,128)S(1)} %fusion.38), channel_id=1, source_target_pairs={{0,16},{16,32},{32,48},{48,64},{64,80},{80,96},{96,112},{112,128},... | collective-permute-start | bytes 221192 | tf_op jit(solution)/shard_map/while/body/eval_jaxpr/ppermute | solution.py:12
  711.1 24.6 %collective-permute-start.1 = (f32[16,1152]{1,0:T(8,128)S(1)}, f32[16,1152]{1,0:T(8,128)S(1)}, u32[]{:S(2)}, u32[]{:S(2)}) collective-permute-start(f32[16,1152]{1,0:T(8,128)S(1)} %fusion.38), channel_id=1, source_target_pairs={{0,16},{16,32},{32,48},{48,64},{64,80},{80,96},{96,112},{112,128},... | collective-permute-start | bytes 221192 | tf_op jit(solution)/shard_map/while/body/eval_jaxpr/ppermute | solution.py:12
  1154.2 24.9 %collective-permute-start.1 = (f32[16,1152]{1,0:T(8,128)S(1)}, f32[16,1152]{1,0:T(8,128)S(1)}, u32[]{:S(2)}, u32[]{:S(2)}) collective-permute-start(f32[16,1152]{1,0:T(8,128)S(1)} %fusion.38), channel_id=1, source_target_pairs={{0,16},{16,32},{32,48},{48,64},{64,80},{80,96},{96,112},{112,128},... | collective-permute-start | bytes 221192 | tf_op jit(solution)/shard_map/while/body/eval_jaxpr/ppermute | solution.py:12
  1213.6 24.6 %collective-permute-start.1 = (f32[16,1152]{1,0:T(8,128)S(1)}, f32[16,1152]{1,0:T(8,128)S(1)}, u32[]{:S(2)}, u32[]{:S(2)}) collective-permute-start(f32[16,1152]{1,0:T(8,128)S(1)} %fusion.38), channel_id=1, source_target_pairs={{0,16},{16,32},{32,48},{48,64},{64,80},{80,96},{96,112},{112,128},... | collective-permute-start | bytes 221192 | tf_op jit(solution)/shard_map/while/body/eval_jaxpr/ppermute | solution.py:12
  1272.7 25.3 %collective-permute-start.1 = (f32[16,1152]{1,0:T(8,128)S(1)}, f32[16,1152]{1,0:T(8,128)S(1)}, u32[]{:S(2)}, u32[]{:S(2)}) collective-permute-start(f32[16,1152]{1,0:T(8,128)S(1)} %fusion.38), channel_id=1, source_target_pairs={{0,16},{16,32},{32,48},{48,64},{64,80},{80,96},{96,112},{112,128},... | collective-permute-start | bytes 221192 | tf_op jit(solution)/shard_map/while/body/eval_jaxpr/ppermute | solution.py:12
  1332.5 24.6 %collective-permute-start.1 = (f32[16,1152]{1,0:T(8,128)S(1)}, f32[16,1152]{1,0:T(8,128)S(1)}, u32[]{:S(2)}, u32[]{:S(2)}) collective-permute-start(f32[16,1152]{1,0:T(8,128)S(1)} %fusion.38), channel_id=1, source_target_pairs={{0,16},{16,32},{32,48},{48,64},{64,80},{80,96},{96,112},{112,128},... | collective-permute-start | bytes 221192 | tf_op jit(solution)/shard_map/while/body/eval_jaxpr/ppermute | solution.py:12
  (106 other events, 2460.6 us)
Sparse Core Ops, SparseCore 0:
  1862.0 201.2 reduce-scatter.1
where the time goes:
time: 2080 us; the launch traced here: 2070 us
  waiting for transfers between devices  1590 us (76%)
  starting transfers between devices  255 us (12%)
  matrix products  197 us (9%)
    ppermute x128, waiting for transfers between devices, shifted(): return lax.ppermute(value, axis, pairs)  1390 us
    ppermute x128, starting transfers between devices, shifted(): return lax.ppermute(value, axis, pairs)  255 us
    reduce_scatter x1, waiting for transfers between devices, per_device(): lax.psum_scatter(image_grad.astype(jnp.bfloat16), ('section', 'mp'), scat...  200 us
    dot_general x64, matrix products, visit(): jnp.dot(block, image_low.T, preferred_element_type=jnp.float32)  140 us
    dot_general x64, matrix products, visit(): jnp.dot(dlogit, image_low, preferred_element_type=jnp.float32)  53.6 us
  transfers between devices with their start and end apart: 129, of which 127 were waited for; matrix products, arithmetic and copies ran while one was open for 9% of the time, Pallas kernels for 0%

commit v1 on v0

v1 whole, which is shorter than its diff:
```python
import functools

import jax
import jax.numpy as jnp
from jax import lax
from jax.experimental import pallas as pl
from jax.experimental.pallas import tpu as pltpu
from jax.sharding import PartitionSpec as P

epsilon = 1e-06
MESH = pl.DeviceIdType.MESH
F32 = jnp.float32
BF16 = jnp.bfloat16

RING = 4
HALVES = 2
CORES = 2


def unit_rows(values):
    widened = values.astype(F32)
    scaling = lax.rsqrt(jnp.sum(widened * widened, axis=-1, keepdims=True) + epsilon)
    return (widened * scaling, scaling)


def unit_backward(unit, scaling, gradient):
    return (gradient - unit * jnp.sum(unit * gradient, axis=-1, keepdims=True)) * scaling


class Plan:
    def __init__(self, send_sems, recv_sems):
        self.send_sems = send_sems
        self.recv_sems = recv_sems
        self.numbers = {}
        self.sends = []

    def number(self, key):
        return self.numbers.setdefault(key, len(self.numbers))

    def copy(self, key, source, target, device):
        at = self.number(key)
        return pltpu.make_async_remote_copy(
            src_ref=source,
            dst_ref=target,
            send_sem=self.send_sems.at[at],
            recv_sem=self.recv_sems.at[at],
            device_id=device,
            device_id_type=MESH,
        )

    def send(self, key, source, target, device):
        copy = self.copy(key, source, target, device)
        copy.start()
        self.sends.append(copy)

    def arrive(self, key, target, device):
        self.copy(key, target, target, device).wait_recv()

    def finish(self):
        for copy in self.sends:
            copy.wait_send()


MOST_COPIES = 96


def kernel(
    zlo_size,
    scale_ref,
    bias_ref,
    image_ref,
    text_ref,
    grad_image_ref,
    grad_text_ref,
    images,
    texts,
    dlogits,
    partial,
    up_out,
    up_in,
    down_out,
    down_in,
    core_out,
    core_in,
    held,
    outer_out,
    first_next,
    first_prev,
    last_next,
    last_prev,
    inner_sum,
    inner_out,
    inner_first,
    inner_next,
    inner_prev,
    half_sum,
    half_out,
    half_in,
    send_sems,
    recv_sems,
):
    rows = text_ref.shape[0]
    width = text_ref.shape[1]
    blocks = zlo_size
    ups = blocks // 2
    downs = blocks - 1 - ups
    group = RING * RING * rows
    z_size = zlo_size * HALVES

    loss = lax.axis_index("loss")
    y = lax.axis_index("section")
    mp = lax.axis_index("mp")
    z_lo = lax.div(loss, RING)
    x = lax.rem(loss, RING)
    z_half = lax.div(mp, CORES)
    core = lax.rem(mp, CORES)
    z = z_half * zlo_size + z_lo

    def device(x_at, y_at, z_at, core_at):
        return {
            "loss": lax.rem(z_at, zlo_size) * RING + x_at,
            "section": y_at,
            "mp": lax.div(z_at, zlo_size) * CORES + core_at,
        }

    def ring(at, steps):
        return lax.rem(at + (steps + RING), RING)

    z_up = device(x, y, lax.rem(z + 1, z_size), core)
    z_down = device(x, y, lax.rem(z + (z_size - 1), z_size), core)
    z_far = device(x, y, lax.rem(z + zlo_size, z_size), core)
    x_next = device(ring(x, 1), y, z, core)
    x_prev = device(ring(x, -1), y, z, core)
    y_next = device(x, ring(y, 1), z, core)
    y_prev = device(x, ring(y, -1), z, core)
    other_core = 1 - core
    sibling = device(x, y, z, other_core)
    neighbours = (z_up, z_down, z_far, x_next, x_prev, y_next, y_prev, sibling)

    barrier = pltpu.get_barrier_semaphore()
    for neighbour in neighbours:
        pl.semaphore_signal(barrier, inc=1, device_id=neighbour, device_id_type=MESH)

    plan = Plan(send_sems, recv_sems)
    unit_text, text_scaling = unit_rows(text_ref[...])
    texts[0] = unit_text.astype(BF16)

    pl.semaphore_wait(barrier, len(neighbours))

    def slot_up(hop):
        return 0 if hop == 0 else 2 * hop - 1

    def slot_down(hop):
        return 2 * hop

    def text_up(hop):
        plan.send(("tu", hop), texts.at[slot_up(hop - 1)], texts.at[slot_up(hop)], z_up)

    def text_down(hop):
        plan.send(("td", hop), texts.at[slot_down(hop - 1)], texts.at[slot_down(hop)], z_down)

    def text_hop(hop):
        plan.arrive(("tu", hop), texts.at[slot_up(hop)], z_up)
        if hop < ups:
            text_up(hop + 1)
        if hop <= downs:
            plan.arrive(("td", hop), texts.at[slot_down(hop)], z_down)
            if hop < downs:
                text_down(hop + 1)

    text_up(1)
    if downs >= 1:
        text_down(1)

    for y_at in range(RING):
        for half_at in range(HALVES):
            for core_at in range(CORES):
                start = ((y_at * HALVES + half_at) * CORES + core_at) * rows
                low = unit_rows(image_ref[start : start + rows, :])[0].astype(BF16)
                if half_at == 0:
                    images[core_at, 0, x, y_at] = low
                else:
                    images[core_at, 1, y_at, x] = low

    def piece(half_at, core_at, x_at):
        if half_at == 0:
            return images.at[core_at, 0, x_at]
        return images.at[core_at, 1, :, x_at]

    for half_at in range(HALVES):
        own = piece(half_at, core, x)
        plan.send(("xn", half_at), own, own, x_next)
        plan.send(("xp", half_at), own, own, x_prev)

    def to_sibling(half_at, steps):
        mine = piece(half_at, core, ring(x, steps))
        plan.send(("xc", half_at, steps), mine, mine, sibling)

    def image_near(half_at):
        from_prev = piece(half_at, core, ring(x, -1))
        from_next = piece(half_at, core, ring(x, 1))
        plan.arrive(("xn", half_at), from_prev, x_next)
        if half_at == 0:
            plan.send(("xf", 0), from_prev, from_prev, x_next)
        plan.arrive(("xp", half_at), from_next, x_prev)
        if half_at == 1:
            plan.send(("xf", 1), from_next, from_next, x_prev)
        to_sibling(half_at, -1)
        to_sibling(half_at, 1)

    def image_far(half_at):
        plan.arrive(("xf", half_at), piece(half_at, core, ring(x, 2)), x_next)
        to_sibling(half_at, 2)

    def image_rest():
        for half_at in range(HALVES):
            for steps in (-1, 1, 2):
                theirs = piece(half_at, other_core, ring(x, steps))
                plan.arrive(("xc", half_at, steps), theirs, sibling)

    scale = scale_ref[0, 0]
    bias = bias_ref[0, 0]
    image_count = CORES * HALVES * group
    own_inner = jnp.where(z_half == 0, x * RING + y, y * RING + x)
    own_start = (core * HALVES + z_half) * group + own_inner * rows

    def batch(first, last):
        count = (last - first) * rows
        block = texts[first:last].reshape(count, width)
        every = images[...].reshape(image_count, width)
        logits = scale * lax.dot_general(
            block, every, (((1,), (1,)), ((), ())), preferred_element_type=F32
        )
        slope = jax.nn.sigmoid(logits + bias)
        if first == 0:
            text_ids = lax.broadcasted_iota(jnp.int32, (count, image_count), 0)
            image_ids = lax.broadcasted_iota(jnp.int32, (count, image_count), 1)
            positive = (text_ids < rows) & (image_ids == text_ids + own_start)
            slope = slope - jnp.where(positive, 1.0, 0.0)
        low = slope.astype(BF16)
        for core_at in range(CORES):
            for half_at in range(HALVES):
                start = (core_at * HALVES + half_at) * group
                dlogits[core_at, half_at, first * rows : last * rows, :] = low[:, start : start + group]
        grads = jnp.dot(low, every, preferred_element_type=F32)
        partial[first:last] = grads.reshape(last - first, rows, width)

    far_at = min(5, ups)
    cuts = {}
    if ups >= 8:
        cuts = {ups - 2: (0, 2 * (ups - 4) + 1), ups - 1: (2 * (ups - 4) + 1, 2 * (ups - 2) + 1), ups: (2 * (ups - 2) + 1, blocks)}
    else:
        cuts = {ups: (0, blocks)}
    images_ready = False
    for hop in range(1, ups + 1):
        text_hop(hop)
        if hop == min(2, ups):
            image_near(0)
        if hop == min(3, ups):
            image_near(1)
        if hop == far_at:
            image_far(0)
            image_far(1)
        if hop in cuts:
            if not images_ready:
                image_rest()
                images_ready = True
            batch(*cuts[hop])

    def back_down(step):
        slot = slot_up(ups + 1 - step)
        total = partial[slot]
        if step > 1:
            plan.arrive(("bd", step - 1), down_in.at[step - 2], z_down)
            total = total + down_in[step - 2].astype(F32)
        down_out[step - 1] = total.astype(BF16)
        plan.send(("bd", step), down_out.at[step - 1], down_in.at[step - 1], z_down)

    def back_up(step):
        slot = slot_down(downs + 1 - step)
        total = partial[slot]
        if step > 1:
            plan.arrive(("bu", step - 1), up_in.at[step - 2], z_up)
            total = total + up_in[step - 2].astype(F32)
        up_out[step - 1] = total.astype(BF16)
        plan.send(("bu", step), up_out.at[step - 1], up_in.at[step - 1], z_up)

    back_steps = iter(range(1, ups + 1))

    def back():
        step = next(back_steps, None)
        if step is None:
            return
        back_down(step)
        if step <= downs:
            back_up(step)

    def image_partial(core_at, half_at):
        every = texts[...].reshape(blocks * rows, width)
        total = lax.dot_general(
            dlogits[core_at, half_at], every, (((0,), (0,)), ((), ())), preferred_element_type=F32
        )
        return total.reshape(RING, RING, rows, width)

    back()
    for half_at in range(HALVES):
        core_out[half_at] = image_partial(other_core, half_at).astype(BF16)
        plan.send(("c", half_at), core_out.at[half_at], core_in.at[half_at], sibling)
    back()
    for half_at in range(HALVES):
        held[half_at] = image_partial(core, half_at)

    outer_at = (x, y)
    inner_at = (y, x)
    outer_next, outer_prev = (x_next, y_next), (x_prev, y_prev)
    inner_up, inner_down = (y_next, x_next), (y_prev, x_prev)

    def summed(half_at, outer, first=0, last=RING):
        return held[half_at, outer, first:last] + core_in[half_at, outer, first:last].astype(F32)

    def outer_start(half_at):
        plan.arrive(("c", half_at), core_in.at[half_at], sibling)
        at = outer_at[half_at]
        far, near, back_at = ring(at, 2), ring(at, 1), ring(at, -1)
        nxt, prv = outer_next[half_at], outer_prev[half_at]
        outer_out[half_at, far] = summed(half_at, far).astype(BF16)
        plan.send(("o1n", half_at), outer_out.at[half_at, far, 0:2], first_next.at[half_at], nxt)
        plan.send(("o1p", half_at), outer_out.at[half_at, far, 2:4], first_prev.at[half_at], prv)
        outer_out[half_at, near, 2:4] = summed(half_at, near, 2, 4).astype(BF16)
        plan.send(("o2n", half_at, 1), outer_out.at[half_at, near, 2:4], last_next.at[half_at, 2:4], nxt)
        outer_out[half_at, back_at, 0:2] = summed(half_at, back_at, 0, 2).astype(BF16)
        plan.send(("o2p", half_at, 0), outer_out.at[half_at, back_at, 0:2], last_prev.at[half_at, 0:2], prv)

    def outer_second(half_at):
        at = outer_at[half_at]
        near, back_at = ring(at, 1), ring(at, -1)
        nxt, prv = outer_next[half_at], outer_prev[half_at]
        plan.arrive(("o1n", half_at), first_next.at[half_at], nxt)
        outer_out[half_at, near, 0:2] = (summed(half_at, near, 0, 2) + first_next[half_at].astype(F32)).astype(BF16)
        plan.send(("o2n", half_at, 0), outer_out.at[half_at, near, 0:2], last_next.at[half_at, 0:2], nxt)
        plan.arrive(("o1p", half_at), first_prev.at[half_at], prv)
        outer_out[half_at, back_at, 2:4] = (summed(half_at, back_at, 2, 4) + first_prev[half_at].astype(F32)).astype(BF16)
        plan.send(("o2p", half_at, 1), outer_out.at[half_at, back_at, 2:4], last_prev.at[half_at, 2:4], prv)

    def inner_start(half_at):
        nxt, prv = outer_next[half_at], outer_prev[half_at]
        for part in (1, 0):
            rng = slice(2 * part, 2 * part + 2)
            plan.arrive(("o2n", half_at, part), last_next.at[half_at, rng], nxt)
            plan.arrive(("o2p", half_at, 1 - part), last_prev.at[half_at, 2 - 2 * part : 4 - 2 * part], prv)
        total = summed(half_at, outer_at[half_at])
        total = total + last_next[half_at].astype(F32) + last_prev[half_at].astype(F32)
        inner_sum[half_at] = total
        at = inner_at[half_at]
        step = 1 if half_at == 0 else -1
        ahead = inner_up[half_at] if half_at == 0 else inner_down[half_at]
        behind = inner_down[half_at] if half_at == 0 else inner_up[half_at]
        inner_out[half_at] = total.astype(BF16)
        plan.send(("i1", half_at), inner_out.at[half_at, ring(at, 2)], inner_first.at[half_at], ahead)
        plan.send(("i2b", half_at), inner_out.at[half_at, ring(at, -step)], inner_prev.at[half_at], behind)

    def inner_second(half_at):
        at = inner_at[half_at]
        step = 1 if half_at == 0 else -1
        ahead = inner_up[half_at] if half_at == 0 else inner_down[half_at]
        near = ring(at, step)
        plan.arrive(("i1", half_at), inner_first.at[half_at], ahead)
        inner_out[half_at, near] = (inner_sum[half_at, near] + inner_first[half_at].astype(F32)).astype(BF16)
        plan.send(("i2a", half_at), inner_out.at[half_at, near], inner_next.at[half_at], ahead)

    def inner_end(half_at):
        ahead = inner_up[half_at] if half_at == 0 else inner_down[half_at]
        behind = inner_down[half_at] if half_at == 0 else inner_up[half_at]
        plan.arrive(("i2b", half_at), inner_prev.at[half_at], behind)
        plan.arrive(("i2a", half_at), inner_next.at[half_at], ahead)
        total = inner_sum[half_at, inner_at[half_at]]
        total = total + inner_prev[half_at].astype(F32) + inner_next[half_at].astype(F32)
        half_sum[half_at] = total
        half_out[half_at] = total.astype(BF16)

    back()
    outer_start(0)
    outer_start(1)
    back()
    outer_second(0)
    outer_second(1)
    back()
    inner_start(0)
    inner_start(1)
    back()
    inner_second(0)
    inner_second(1)
    back()
    inner_end(0)
    inner_end(1)
    plan.send(("h",), half_out.at[1 - z_half], half_in, z_far)
    for _ in range(ups):
        back()

    plan.arrive(("bd", ups), down_in.at[ups - 1], z_down)
    total = partial[0] + down_in[ups - 1].astype(F32)
    if downs >= 1:
        plan.arrive(("bu", downs), up_in.at[downs - 1], z_up)
        total = total + up_in[downs - 1].astype(F32)
    unit_text, text_scaling = unit_rows(text_ref[...])
    grad_text_ref[...] = unit_backward(unit_text, text_scaling, scale * total)

    own_row = pl.multiple_of(((y * HALVES + z_half) * CORES + core) * rows, rows)
    unit_image, image_scaling = unit_rows(image_ref[pl.ds(own_row, rows), :])
    plan.arrive(("h",), half_in, z_far)
    total = half_sum[z_half] + half_in[...].astype(F32)
    grad_image_ref[...] = unit_backward(unit_image, image_scaling, scale * total)
    plan.finish()


def per_device(image_embed, text_embed, logit_scale, logit_bias):
    rows, width = text_embed.shape
    zlo_size = lax.axis_size("loss") // RING
    blocks = zlo_size
    ups = blocks // 2
    downs = max(blocks - 1 - ups, 1)
    group = RING * RING * rows

    def scratch(*shape, dtype=BF16):
        return pltpu.VMEM((*shape, rows, width), dtype)

    smem = pl.BlockSpec(memory_space=pltpu.SMEM)
    vmem = pl.BlockSpec(memory_space=pltpu.VMEM)
    return pl.pallas_call(
        functools.partial(kernel, zlo_size),
        out_shape=[jax.ShapeDtypeStruct((rows, width), F32)] * 2,
        in_specs=[smem, smem, vmem, vmem],
        out_specs=[vmem, vmem],
        scratch_shapes=[
            scratch(CORES, HALVES, RING, RING),
            scratch(blocks),
            pltpu.VMEM((CORES, HALVES, blocks * rows, group), BF16),
            scratch(blocks, dtype=F32),
            scratch(downs),
            scratch(downs),
            scratch(ups),
            scratch(ups),
            scratch(HALVES, RING, RING),
            scratch(HALVES, RING, RING),
            scratch(HALVES, RING, RING, dtype=F32),
            scratch(HALVES, RING, RING),
            scratch(HALVES, 2),
            scratch(HALVES, 2),
            scratch(HALVES, RING),
            scratch(HALVES, RING),
            scratch(HALVES, RING, dtype=F32),
            scratch(HALVES, RING),
            scratch(HALVES),
            scratch(HALVES),
            scratch(HALVES),
            scratch(HALVES, dtype=F32),
            scratch(HALVES),
            scratch(),
            pltpu.SemaphoreType.DMA((MOST_COPIES,)),
            pltpu.SemaphoreType.DMA((MOST_COPIES,)),
        ],
        compiler_params=pltpu.CompilerParams(
            collective_id=0, has_side_effects=True, vmem_limit_bytes=48 * 1024 * 1024
        ),
    )(logit_scale.reshape(1, 1), logit_bias.reshape(1, 1), image_embed, text_embed)


def solution(mesh):
    placed = (P("loss", None), P(("loss", "section", "mp"), None), P(), P())
    return jax.shard_map(
        per_device,
        mesh=mesh,
        in_specs=placed,
        out_specs=(P(("loss", "section", "mp"), None), P(("loss", "section", "mp"), None)),
        check_vma=False,
    )
```

time: 2080 us -> 96.6 us (0.05)
  waiting for transfers between devices: 1590 us -> 0 us
  starting transfers between devices: 255 us -> 0 us
  matrix products: 197 us -> 0 us
  Pallas kernels: 0 us -> 90.3 us
    ppermute x128 -> x0, waiting for transfers between devices: 1390 us -> none  [shifted(): return lax.ppermute(value, axis, pairs)]
    ppermute x128 -> x0, starting transfers between devices: 255 us -> none  [shifted(): return lax.ppermute(value, axis, pairs)]
    reduce_scatter x1 -> x0, waiting for transfers between devices: 200 us -> none  [per_device(): lax.psum_scatter(image_grad.astype(jnp.bfloat16), ('section', 'mp'), scat...]
    dot_general x129 -> x0, matrix products: 197 us -> none  [the longest x64 140 us: visit(): jnp.dot(block, image_low.T, preferred_element_type=jnp.float32)]
    pallas_call x0 -> x1, Pallas kernels: none -> 90.3 us  [per_device(): pl.pallas_call(functools.partial(kernel, zlo_size), out_shape=[jax.ShapeD...]
  transfers between devices with their start and end apart: 129 -> 0, of which waited for: 127 -> 0; matrix products, arithmetic and copies ran while one was open for 9% -> 0% of each run, Pallas kernels for 0% -> 0%
where the time goes in v1:
time: 96.6 us; the launch traced here: 95.3 us
  Pallas kernels  90.3 us (93%)
  local copies, waits for them, and re-layouts  3.09 us (3%)
  between operations  1.94 us (2%)
    pallas_call x1, Pallas kernels, per_device(): pl.pallas_call(functools.partial(kernel, zlo_size), out_shape=[jax.ShapeD...  90.3 us
    unnamed x6, local copies, waits for them, and re-layouts  3.09 us

profile of v1, /device:TPU:6, one launch (start us, length us, event | category | flops | bytes accessed | tf_op | source)
XLA Modules:
  0.0 95.3 jit_solution(7637967681553675111)
XLA Ops:
  1.9 0.0 copy-start
  1.9 1.1 %copy-done = bf16[256,1152]{1,0:T(8,128)(2,1)S(1)} copy-done((bf16[256,1152]{1,0:T(8,128)(2,1)S(1)}, bf16[256,1152]{1,0:T(8,128)(2,1)}, u32[]{:S(2)}) %copy-start) | copy-done | bytes 589848
  3.0 0.0 copy-start.1
  3.0 0.8 copy-done.1
  3.8 90.3 %shard_map.59 = (f32[16,1152]{1,0:T(8,128)S(1)}, f32[16,1152]{1,0:T(8,128)S(1)}) custom-call(f32[1,1]{1,0:T(1,128)} %bitcast.2.scale_ref, f32[1,1]{1,0:T(1,128)} %bitcast.3.bias_ref, bf16[256,1152]{1,0:T(8,128)(2,1)S(1)} %copy-done, bf16[16,1152]{1,0:T(8,128)(2,1)S(1)} %copy-done.1), custom_call_target="tpu_custom_call" | custom-call | tf_op jit(solution)/shard_map/pallas_call | solution.py:429
  94.0 0.6 copy.10
  94.7 0.6 copy.11
Async XLA Ops:
  1.9 1.1 %copy-start = (bf16[256,1152]{1,0:T(8,128)(2,1)S(1)}, bf16[256,1152]{1,0:T(8,128)(2,1)}, u32[]{:S(2)}) copy-start(bf16[256,1152]{1,0:T(8,128)(2,1)} %image_ref.1) | copy-start | bytes 1769476
  3.0 0.8 copy-start.1

commit v2 on v0

v2 whole, which is shorter than its diff:
```python
import functools

import jax
import jax.numpy as jnp
from jax import lax
from jax.experimental import pallas as pl
from jax.experimental.pallas import tpu as pltpu
from jax.sharding import PartitionSpec as P

epsilon = 1e-06
MESH = pl.DeviceIdType.MESH
F32 = jnp.float32
BF16 = jnp.bfloat16

RING = 4
HALVES = 2
CORES = 2
MOST_COPIES = 112

TREE = {0: (3, 1), 3: (6, 4), 1: (2,), 6: (8, 7), 4: (5,)}

X_OWN, X_PREV, X_NEXT, X_FAR = range(4)
Y_OWN, Y_NEXT, Y_FAR, Y_PREV = range(4)


def unit_rows(values):
    widened = values.astype(F32)
    scaling = lax.rsqrt(jnp.sum(widened * widened, axis=-1, keepdims=True) + epsilon)
    return (widened * scaling, scaling)


def unit_backward(unit, scaling, gradient):
    return (gradient - unit * jnp.sum(unit * gradient, axis=-1, keepdims=True)) * scaling


class Plan:
    def __init__(self, send_sems, recv_sems):
        self.send_sems = send_sems
        self.recv_sems = recv_sems
        self.numbers = {}
        self.sends = []

    def copy(self, key, source, target, device):
        at = self.numbers.setdefault(key, len(self.numbers))
        return pltpu.make_async_remote_copy(
            src_ref=source,
            dst_ref=target,
            send_sem=self.send_sems.at[at],
            recv_sem=self.recv_sems.at[at],
            device_id=device,
            device_id_type=MESH,
        )

    def send(self, key, source, target, device):
        copy = self.copy(key, source, target, device)
        copy.start()
        self.sends.append(copy)

    def arrive(self, key, target, device):
        self.copy(key, target, target, device).wait_recv()

    def finish(self):
        for copy in self.sends:
            copy.wait_send()


class Spread:
    def __init__(self, blocks):
        self.reach = (blocks // 2, blocks - 1 - blocks // 2)
        self.parent = {}
        self.levels = []
        level = [0]
        while level:
            found = []
            for at in level:
                for child in TREE.get(at, ()):
                    if child <= max(self.reach):
                        self.parent[child] = at
                        found.append(child)
            level = found
            if found:
                self.levels.append(found)
        self.slots = {(0, 0): 0, (1, 0): 0}
        self.order = []
        for level in self.levels:
            for at in level:
                for way in range(2):
                    if at <= self.reach[way]:
                        self.slots[way, at] = len(self.order) + 1
                        self.order.append((way, at))
        self.lengths = sorted({child - at for child, at in self.parent.items()})

    def children(self, way, at):
        return [child for child in TREE.get(at, ()) if child <= self.reach[way]]


def kernel(
    zlo_size,
    scale_ref,
    bias_ref,
    image_hbm,
    text_hbm,
    grad_image_ref,
    grad_text_ref,
    image_raw,
    text_raw,
    images,
    texts,
    dlogits,
    partial,
    back_out,
    back_in,
    core_out,
    core_in,
    held,
    outer_out,
    first_next,
    first_prev,
    last_next,
    last_prev,
    inner_out,
    inner_in,
    half_sum,
    half_out,
    half_in,
    load_sems,
    send_sems,
    recv_sems,
):
    rows, width = text_raw.shape
    blocks = zlo_size
    spread = Spread(blocks)
    side = RING * CORES * RING * rows
    z_size = zlo_size * HALVES

    loss = lax.axis_index("loss")
    y = lax.axis_index("section")
    mp = lax.axis_index("mp")
    z_lo = lax.div(loss, RING)
    x = lax.rem(loss, RING)
    z_half = lax.div(mp, CORES)
    core = lax.rem(mp, CORES)
    z = z_half * zlo_size + z_lo

    def device(x_steps=0, y_steps=0, z_steps=0, core_steps=0):
        z_at = lax.rem(z + (z_steps + z_size), z_size)
        return {
            "loss": lax.rem(z_at, zlo_size) * RING + lax.rem(x + (x_steps + RING), RING),
            "section": lax.rem(y + (y_steps + RING), RING),
            "mp": lax.div(z_at, zlo_size) * CORES + lax.rem(core + core_steps, CORES),
        }

    z_far = device(z_steps=zlo_size)
    x_next, x_prev, x_far = device(x_steps=1), device(x_steps=-1), device(x_steps=2)
    y_next, y_prev, y_far = device(y_steps=1), device(y_steps=-1), device(y_steps=2)
    sibling = device(core_steps=1)
    along_z = {steps: device(z_steps=steps) for length in spread.lengths for steps in (length, -length)}
    neighbours = [*along_z.values(), x_next, x_prev, x_far, y_next, y_prev, y_far, sibling]

    barrier = pltpu.get_barrier_semaphore()
    for neighbour in neighbours:
        pl.semaphore_signal(barrier, inc=1, device_id=neighbour, device_id_type=MESH)

    load_text = pltpu.make_async_copy(text_hbm, text_raw, load_sems.at[0])
    load_image = pltpu.make_async_copy(image_hbm, image_raw, load_sems.at[1])
    load_text.start()
    load_image.start()

    plan = Plan(send_sems, recv_sems)
    load_text.wait()
    texts[0] = unit_rows(text_raw[...])[0].astype(BF16)

    load_image.wait()

    def normalize(core_steps):
        for half_at in range(HALVES):
            for y_steps in range(RING):
                y_at = lax.rem(y + y_steps, RING)
                half = z_half if half_at == 1 else 1 - z_half
                core_at = lax.rem(core + core_steps, CORES)
                start = pl.multiple_of(((y_at * HALVES + half) * CORES + core_at) * rows, rows)
                low = unit_rows(image_raw[pl.ds(start, rows), :])[0].astype(BF16)
                images[X_OWN, half_at, core_steps, y_steps] = low

    normalize(0)
    pl.semaphore_wait(barrier, len(neighbours))

    def pass_on(way, at):
        for child in spread.children(way, at):
            target = along_z[child - at if way == 0 else at - child]
            source, slot = spread.slots[way, at], spread.slots[way, child]
            plan.send(("t", way, child), texts.at[source], texts.at[slot], target)

    def text_level(level):
        for at in spread.levels[level]:
            for way in range(2):
                if at <= spread.reach[way]:
                    near = spread.lengths[0] * (1 - 2 * way)
                    plan.arrive(("t", way, at), texts.at[spread.slots[way, at]], along_z[near])
                    pass_on(way, at)

    pass_on(0, 0)
    pass_on(1, 0)

    for half_at in range(HALVES):
        own = images.at[X_OWN, half_at, 0]
        plan.send(("xn", half_at), own, images.at[X_PREV, half_at, 0], x_next)
        other = 1 - half_at
        own = images.at[X_OWN, other, 0]
        plan.send(("xp", other), own, images.at[X_NEXT, other, 0], x_prev)

    normalize(1)

    def to_sibling(x_at, half_at):
        mine, theirs = images.at[x_at, half_at, 0], images.at[x_at, half_at, 1]
        plan.send(("xc", x_at, half_at), mine, theirs, sibling)

    def image_near(half_at):
        other = 1 - half_at
        from_prev, from_next = images.at[X_PREV, half_at, 0], images.at[X_NEXT, other, 0]
        plan.arrive(("xn", half_at), from_prev, x_next)
        if half_at == 0:
            plan.send(("xf", 0), from_prev, images.at[X_FAR, 0, 0], x_next)
        plan.arrive(("xp", other), from_next, x_prev)
        if half_at == 0:
            plan.send(("xf", 1), from_next, images.at[X_FAR, 1, 0], x_prev)
        to_sibling(X_PREV, half_at)
        to_sibling(X_NEXT, other)

    def image_far():
        for half_at in range(HALVES):
            plan.arrive(("xf", half_at), images.at[X_FAR, half_at, 0], x_next)
            to_sibling(X_FAR, half_at)

    def from_sibling(*x_ats):
        for half_at in range(HALVES):
            for x_at in x_ats:
                plan.arrive(("xc", x_at, half_at), images.at[x_at, half_at, 1], sibling)

    scale = scale_ref[0, 0]
    bias = bias_ref[0, 0]
    per_x = HALVES * CORES * RING * rows
    per_half = CORES * RING * rows

    def batch(first, last):
        count = (last - first) * per_x
        block = texts[...].reshape(blocks * rows, width)
        every = images[first:last].reshape(count, width)
        logits = scale * lax.dot_general(
            block, every, (((1,), (1,)), ((), ())), preferred_element_type=F32
        )
        slope = jax.nn.sigmoid(logits + bias)
        if first == X_OWN:
            text_ids = lax.broadcasted_iota(jnp.int32, slope.shape, 0)
            image_ids = lax.broadcasted_iota(jnp.int32, slope.shape, 1)
            positive = (text_ids < rows) & (image_ids == text_ids + per_half)
            slope = slope - jnp.where(positive, 1.0, 0.0)
        low = slope.astype(BF16)
        for x_at in range(first, last):
            for half_at in range(HALVES):
                start = (x_at - first) * per_x + half_at * per_half
                dlogits[half_at, :, x_at * per_half : (x_at + 1) * per_half] = low[:, start : start + per_half]
        grads = jnp.dot(low, every, preferred_element_type=F32).reshape(blocks, rows, width)
        if first == X_OWN:
            partial[...] = grads
        else:
            partial[...] += grads

    text_level(0)
    image_near(0)
    for level in range(1, len(spread.levels)):
        text_level(level)
        if level == 1:
            image_near(1)
    image_far()
    from_sibling(X_PREV, X_NEXT)
    batch(X_OWN, X_FAR)
    from_sibling(X_FAR)
    batch(X_FAR, X_FAR + 1)

    def back(level):
        for at in reversed(spread.levels[level]):
            for way in range(2):
                if at <= spread.reach[way]:
                    slot = spread.slots[way, at]
                    total = partial[slot]
                    for child in spread.children(way, at):
                        total = total + back_arrival(way, child)
                    back_out[slot] = total.astype(BF16)
                    length = at - spread.parent[at]
                    target = along_z[length if way == 1 else -length]
                    plan.send(("b", way, at), back_out.at[slot], back_in.at[slot], target)

    def back_arrival(way, child):
        slot = spread.slots[way, child]
        near = spread.lengths[0] * (2 * way - 1)
        plan.arrive(("b", way, child), back_in.at[slot], along_z[near])
        return back_in[slot].astype(F32)

    def image_partial(half_at):
        every = texts[...].reshape(blocks * rows, width)
        total = lax.dot_general(
            dlogits[half_at], every, (((0,), (0,)), ((), ())), preferred_element_type=F32
        )
        total = total.reshape(RING, CORES, RING, rows, width)
        core_out[half_at] = total[:, 1].astype(BF16)
        plan.send(("c", half_at), core_out.at[half_at], core_in.at[half_at], sibling)
        held[half_at] = total[:, 0]

    split = (width // 128 + 1) // 2 * 128
    columns = (slice(0, split), slice(split, width))
    ahead, behind = (x_next, y_next), (x_prev, y_prev)
    positions = ((X_OWN, X_NEXT, X_FAR, X_PREV), (Y_OWN, Y_NEXT, Y_FAR, Y_PREV))

    def at_block(half_at, part, outer, first=0, last=RING):
        if part == 0:
            return (half_at, outer, slice(first, last), slice(None), columns[0])
        return (half_at, slice(first, last), outer, slice(None), columns[1])

    def at_line(half_at, part, first=0, last=RING):
        return (half_at, slice(first, last), slice(None), columns[part])

    def send_block(key, half_at, part, outer, first, last, target, target_at, to):
        source = outer_out.at[at_block(half_at, part, outer, first, last)]
        plan.send((key, half_at, part, first), source, target.at[target_at], to)

    def summed(index):
        return held[index] + core_in[index].astype(F32)

    def outer_start(half_at):
        plan.arrive(("c", half_at), core_in.at[half_at], sibling)
        for part in range(2):
            _, nxt, far, prv = positions[part]
            index = at_block(half_at, part, far)
            outer_out[index] = summed(index).astype(BF16)
            line = at_line(half_at, part, 0, 2)
            send_block("o1n", half_at, part, far, 0, 2, first_next, line, ahead[part])
            send_block("o1p", half_at, part, far, 2, 4, first_prev, line, behind[part])
        for part in range(2):
            _, nxt, far, prv = positions[part]
            index = at_block(half_at, part, nxt, 2, 4)
            outer_out[index] = summed(index).astype(BF16)
            send_block("o2n", half_at, part, nxt, 2, 4, last_next, at_line(half_at, part, 2, 4), ahead[part])
            index = at_block(half_at, part, prv, 0, 2)
            outer_out[index] = summed(index).astype(BF16)
            send_block("o2p", half_at, part, prv, 0, 2, last_prev, at_line(half_at, part, 0, 2), behind[part])

    def outer_second(half_at):
        for part in range(2):
            _, nxt, far, prv = positions[part]
            line = at_line(half_at, part, 0, 2)
            plan.arrive(("o1n", half_at, part, 0), first_next.at[line], ahead[part])
            index = at_block(half_at, part, nxt, 0, 2)
            outer_out[index] = (summed(index) + first_next[line].astype(F32)).astype(BF16)
            send_block("o2n", half_at, part, nxt, 0, 2, last_next, line, ahead[part])
            plan.arrive(("o1p", half_at, part, 2), first_prev.at[line], behind[part])
            index = at_block(half_at, part, prv, 2, 4)
            outer_out[index] = (summed(index) + first_prev[line].astype(F32)).astype(BF16)
            send_block("o2p", half_at, part, prv, 2, 4, last_prev, at_line(half_at, part, 2, 4), behind[part])

    inner_targets = (
        ((Y_FAR, y_far), (Y_NEXT, y_next), (Y_PREV, y_prev)),
        ((X_FAR, x_far), (X_NEXT, x_next), (X_PREV, x_prev)),
    )

    def inner_start(half_at):
        for part in range(2):
            for first in (2, 0):
                line = at_line(half_at, part, first, first + 2)
                plan.arrive(("o2n", half_at, part, first), last_next.at[line], ahead[part])
            for first in (0, 2):
                line = at_line(half_at, part, first, first + 2)
                plan.arrive(("o2p", half_at, part, first), last_prev.at[line], behind[part])
            line = at_line(half_at, part)
            total = summed(at_block(half_at, part, 0))
            total = total + last_next[line].astype(F32) + last_prev[line].astype(F32)
            inner_out[line] = total.astype(BF16)
            for at, to in inner_targets[part]:
                block = (half_at, at, slice(None), columns[part])
                plan.send(("i", half_at, part, at), inner_out.at[block], inner_in.at[block], to)
            half_sum[half_at, :, columns[part]] = total[0]

    def inner_end(half_at):
        for part in range(2):
            total = half_sum[half_at, :, columns[part]]
            for at, to in inner_targets[part]:
                block = (half_at, at, slice(None), columns[part])
                plan.arrive(("i", half_at, part, at), inner_in.at[block], to)
                total = total + inner_in[block].astype(F32)
            if half_at == 0:
                half_out[:, columns[part]] = total.astype(BF16)
            else:
                half_sum[half_at, :, columns[part]] = total

    last = len(spread.levels) - 1
    back(last)
    image_partial(0)
    image_partial(1)
    outer_start(0)
    for level in range(last - 1, 0, -1):
        back(level)
    outer_second(0)
    outer_start(1)
    if last > 0:
        back(0)
    inner_start(0)
    outer_second(1)

    total = partial[0]
    for way in range(2):
        for child in spread.children(way, 0):
            total = total + back_arrival(way, child)
    inner_end(0)
    plan.send(("h",), half_out, half_in, z_far)
    unit_text, text_scaling = unit_rows(text_raw[...])
    grad_text_ref[...] = unit_backward(unit_text, text_scaling, scale * total)

    inner_start(1)
    inner_end(1)
    own_row = pl.multiple_of(((y * HALVES + z_half) * CORES + core) * rows, rows)
    unit_image, image_scaling = unit_rows(image_raw[pl.ds(own_row, rows), :])
    plan.arrive(("h",), half_in, z_far)
    total = half_sum[1] + half_in[...].astype(F32)
    grad_image_ref[...] = unit_backward(unit_image, image_scaling, scale * total)
    plan.finish()


def per_device(image_embed, text_embed, logit_scale, logit_bias):
    rows, width = text_embed.shape
    zlo_size = lax.axis_size("loss") // RING
    blocks = zlo_size

    def scratch(*shape, dtype=BF16):
        return pltpu.VMEM((*shape, rows, width), dtype)

    smem = pl.BlockSpec(memory_space=pltpu.SMEM)
    vmem = pl.BlockSpec(memory_space=pltpu.VMEM)
    anywhere = pl.BlockSpec(memory_space=pl.ANY)
    return pl.pallas_call(
        functools.partial(kernel, zlo_size),
        out_shape=[jax.ShapeDtypeStruct((rows, width), F32)] * 2,
        in_specs=[smem, smem, anywhere, anywhere],
        out_specs=[vmem, vmem],
        scratch_shapes=[
            pltpu.VMEM(image_embed.shape, BF16),
            pltpu.VMEM(text_embed.shape, BF16),
            scratch(RING, HALVES, CORES, RING),
            scratch(blocks),
            pltpu.VMEM((HALVES, blocks * rows, RING * CORES * RING * rows), BF16),
            scratch(blocks, dtype=F32),
            scratch(blocks),
            scratch(blocks),
            scratch(HALVES, RING, RING),
            scratch(HALVES, RING, RING),
            scratch(HALVES, RING, RING, dtype=F32),
            scratch(HALVES, RING, RING),
            scratch(HALVES, 2),
            scratch(HALVES, 2),
            scratch(HALVES, RING),
            scratch(HALVES, RING),
            scratch(HALVES, RING),
            scratch(HALVES, RING),
            scratch(HALVES, dtype=F32),
            scratch(),
            scratch(),
            pltpu.SemaphoreType.DMA((2,)),
            pltpu.SemaphoreType.DMA((MOST_COPIES,)),
            pltpu.SemaphoreType.DMA((MOST_COPIES,)),
        ],
        compiler_params=pltpu.CompilerParams(
            collective_id=0, has_side_effects=True, vmem_limit_bytes=60 * 1024 * 1024
        ),
    )(logit_scale.reshape(1, 1), logit_bias.reshape(1, 1), image_embed, text_embed)


def solution(mesh):
    placed = (P("loss", None), P(("loss", "section", "mp"), None), P(), P())
    return jax.shard_map(
        per_device,
        mesh=mesh,
        in_specs=placed,
        out_specs=(P(("loss", "section", "mp"), None), P(("loss", "section", "mp"), None)),
        check_vma=False,
    )
```

time: 2080 us -> 73.7 us (0.04)
  waiting for transfers between devices: 1590 us -> 0 us
  starting transfers between devices: 255 us -> 0 us
  matrix products: 197 us -> 0 us
  Pallas kernels: 0 us -> 69.3 us
    ppermute x128 -> x0, waiting for transfers between devices: 1390 us -> none  [shifted(): return lax.ppermute(value, axis, pairs)]
    ppermute x128 -> x0, starting transfers between devices: 255 us -> none  [shifted(): return lax.ppermute(value, axis, pairs)]
    reduce_scatter x1 -> x0, waiting for transfers between devices: 200 us -> none  [per_device(): lax.psum_scatter(image_grad.astype(jnp.bfloat16), ('section', 'mp'), scat...]
    dot_general x129 -> x0, matrix products: 197 us -> none  [the longest x64 140 us: visit(): jnp.dot(block, image_low.T, preferred_element_type=jnp.float32)]
    pallas_call x0 -> x1, Pallas kernels: none -> 69.3 us  [per_device(): pl.pallas_call(functools.partial(kernel, zlo_size), out_shape=[jax.ShapeD...]
  transfers between devices with their start and end apart: 129 -> 0, of which waited for: 127 -> 0; matrix products, arithmetic and copies ran while one was open for 9% -> 0% of each run, Pallas kernels for 0% -> 0%
where the time goes in v2:
time: 73.7 us; the launch traced here: 73.4 us
  Pallas kernels  69.3 us (94%)
  local copies, waits for them, and re-layouts  2.19 us (3%)
  between operations  1.94 us (3%)
    pallas_call x1, Pallas kernels, per_device(): pl.pallas_call(functools.partial(kernel, zlo_size), out_shape=[jax.ShapeD...  69.3 us
    unnamed x4, local copies, waits for them, and re-layouts  2.19 us

profile of v2, /device:TPU:6, one launch (start us, length us, event | category | flops | bytes accessed | tf_op | source)
XLA Modules:
  0.0 73.4 jit_solution(4537094182675940201)
XLA Ops:
  1.9 69.3 %shard_map.59 = (f32[16,1152]{1,0:T(8,128)}, f32[16,1152]{1,0:T(8,128)}) custom-call(f32[1,1]{1,0:T(1,128)} %bitcast.2.scale_ref, f32[1,1]{1,0:T(1,128)} %bitcast.3.bias_ref, bf16[256,1152]{1,0:T(8,128)(2,1)} %image_hbm.1, bf16[16,1152]{1,0:T(8,128)(2,1)} %text_hbm.1), custom_call_target="tpu_custom_call" | custom-call | tf_op jit(solution)/shard_map/pallas_call | solution.py:439
  71.2 0.0 copy-start
  71.2 1.6 %copy.10 = f32[16,1152]{1,0:T(8,128)} copy(f32[16,1152]{1,0:T(8,128)} %get-tuple-element.4) | data formatting | bytes 147456
  72.8 0.0 copy-done
  72.8 0.6 copy.11
Async XLA Ops:
  71.2 1.6 %copy-start = (f32[16,1152]{1,0:T(8,128)S(1)}, f32[16,1152]{1,0:T(8,128)}, u32[]{:S(2)}) copy-start(f32[16,1152]{1,0:T(8,128)} %get-tuple-element.5) | copy-start | bytes 221188

commit v3 on v2

--- a/solution.py
+++ b/solution.py
@@ -114,16 +114,14 @@
     core_in,
     held,
     outer_out,
-    first_next,
-    first_prev,
-    last_next,
-    last_prev,
+    outer_in,
     inner_out,
     inner_in,
     half_sum,
     half_out,
     half_in,
     load_sems,
+    token_sems,
     send_sems,
     recv_sems,
 ):
@@ -169,8 +167,6 @@
     plan = Plan(send_sems, recv_sems)
     load_text.wait()
     texts[0] = unit_rows(text_raw[...])[0].astype(BF16)
-
-    load_image.wait()
 
     def normalize(core_steps):
         for half_at in range(HALVES):
@@ -182,7 +178,6 @@
                 low = unit_rows(image_raw[pl.ds(start, rows), :])[0].astype(BF16)
                 images[X_OWN, half_at, core_steps, y_steps] = low
 
-    normalize(0)
     pl.semaphore_wait(barrier, len(neighbours))
 
     def pass_on(way, at):
@@ -201,6 +196,8 @@
 
     pass_on(0, 0)
     pass_on(1, 0)
+    load_image.wait()
+    normalize(0)
 
     for half_at in range(HALVES):
         own = images.at[X_OWN, half_at, 0]
@@ -242,15 +239,16 @@
     per_x = HALVES * CORES * RING * rows
     per_half = CORES * RING * rows
 
-    def batch(first, last):
+    def batch(slots, first, last):
         count = (last - first) * per_x
-        block = texts[...].reshape(blocks * rows, width)
+        low_row, high_row = slots[0] * rows, slots[1] * rows
+        block = texts[slots[0] : slots[1]].reshape(high_row - low_row, width)
         every = images[first:last].reshape(count, width)
         logits = scale * lax.dot_general(
             block, every, (((1,), (1,)), ((), ())), preferred_element_type=F32
         )
         slope = jax.nn.sigmoid(logits + bias)
-        if first == X_OWN:
+        if first == X_OWN and slots[0] == 0:
             text_ids = lax.broadcasted_iota(jnp.int32, slope.shape, 0)
             image_ids = lax.broadcasted_iota(jnp.int32, slope.shape, 1)
             positive = (text_ids < rows) & (image_ids == text_ids + per_half)
@@ -259,24 +257,13 @@
         for x_at in range(first, last):
             for half_at in range(HALVES):
                 start = (x_at - first) * per_x + half_at * per_half
-                dlogits[half_at, :, x_at * per_half : (x_at + 1) * per_half] = low[:, start : start + per_half]
-        grads = jnp.dot(low, every, preferred_element_type=F32).reshape(blocks, rows, width)
+                part = low[:, start : start + per_half]
+                dlogits[half_at, low_row:high_row, x_at * per_half : (x_at + 1) * per_half] = part
+        grads = jnp.dot(low, every, preferred_element_type=F32).reshape(-1, rows, width)
         if first == X_OWN:
-            partial[...] = grads
+            partial[slots[0] : slots[1]] = grads
         else:
-            partial[...] += grads
-
-    text_level(0)
-    image_near(0)
-    for level in range(1, len(spread.levels)):
-        text_level(level)
-        if level == 1:
-            image_near(1)
-    image_far()
-    from_sibling(X_PREV, X_NEXT)
-    batch(X_OWN, X_FAR)
-    from_sibling(X_FAR)
-    batch(X_FAR, X_FAR + 1)
+            partial[slots[0] : slots[1]] += grads
 
     def back(level):
         for at in reversed(spread.levels[level]):
@@ -309,114 +296,106 @@
 
     split = (width // 128 + 1) // 2 * 128
     columns = (slice(0, split), slice(split, width))
-    ahead, behind = (x_next, y_next), (x_prev, y_prev)
-    positions = ((X_OWN, X_NEXT, X_FAR, X_PREV), (Y_OWN, Y_NEXT, Y_FAR, Y_PREV))
-
-    def at_block(half_at, part, outer, first=0, last=RING):
+    x_targets = ((X_FAR, x_far), (X_NEXT, x_next), (X_PREV, x_prev))
+    y_targets = ((Y_FAR, y_far), (Y_NEXT, y_next), (Y_PREV, y_prev))
+    outer_targets, inner_targets = (x_targets, y_targets), (y_targets, x_targets)
+
+    def at_block(half_at, part, outer):
         if part == 0:
-            return (half_at, outer, slice(first, last), slice(None), columns[0])
-        return (half_at, slice(first, last), outer, slice(None), columns[1])
-
-    def at_line(half_at, part, first=0, last=RING):
-        return (half_at, slice(first, last), slice(None), columns[part])
-
-    def send_block(key, half_at, part, outer, first, last, target, target_at, to):
-        source = outer_out.at[at_block(half_at, part, outer, first, last)]
-        plan.send((key, half_at, part, first), source, target.at[target_at], to)
+            return (half_at, outer, slice(None), slice(None), columns[0])
+        return (half_at, slice(None), outer, slice(None), columns[1])
+
+    def at_line(half_at, part, *at):
+        return (half_at, *at, slice(None), slice(None), columns[part])
 
     def summed(index):
         return held[index] + core_in[index].astype(F32)
 
     def outer_start(half_at):
         plan.arrive(("c", half_at), core_in.at[half_at], sibling)
-        for part in range(2):
-            _, nxt, far, prv = positions[part]
-            index = at_block(half_at, part, far)
-            outer_out[index] = summed(index).astype(BF16)
-            line = at_line(half_at, part, 0, 2)
-            send_block("o1n", half_at, part, far, 0, 2, first_next, line, ahead[part])
-            send_block("o1p", half_at, part, far, 2, 4, first_prev, line, behind[part])
-        for part in range(2):
-            _, nxt, far, prv = positions[part]
-            index = at_block(half_at, part, nxt, 2, 4)
-            outer_out[index] = summed(index).astype(BF16)
-            send_block("o2n", half_at, part, nxt, 2, 4, last_next, at_line(half_at, part, 2, 4), ahead[part])
-            index = at_block(half_at, part, prv, 0, 2)
-            outer_out[index] = summed(index).astype(BF16)
-            send_block("o2p", half_at, part, prv, 0, 2, last_prev, at_line(half_at, part, 0, 2), behind[part])
-
-    def outer_second(half_at):
-        for part in range(2):
-            _, nxt, far, prv = positions[part]
-            line = at_line(half_at, part, 0, 2)
-            plan.arrive(("o1n", half_at, part, 0), first_next.at[line], ahead[part])
-            index = at_block(half_at, part, nxt, 0, 2)
-            outer_out[index] = (summed(index) + first_next[line].astype(F32)).astype(BF16)
-            send_block("o2n", half_at, part, nxt, 0, 2, last_next, line, ahead[part])
-            plan.arrive(("o1p", half_at, part, 2), first_prev.at[line], behind[part])
-            index = at_block(half_at, part, prv, 2, 4)
-            outer_out[index] = (summed(index) + first_prev[line].astype(F32)).astype(BF16)
-            send_block("o2p", half_at, part, prv, 2, 4, last_prev, at_line(half_at, part, 2, 4), behind[part])
-
-    inner_targets = (
-        ((Y_FAR, y_far), (Y_NEXT, y_next), (Y_PREV, y_prev)),
-        ((X_FAR, x_far), (X_NEXT, x_next), (X_PREV, x_prev)),
-    )
+        for way in range(RING - 1):
+            for part in range(2):
+                at, to = outer_targets[part][way]
+                index = at_block(half_at, part, at)
+                outer_out[index] = summed(index).astype(BF16)
+                plan.send(("o", half_at, part, at), outer_out.at[index], outer_in.at[at_line(half_at, part, at)], to)
 
     def inner_start(half_at):
         for part in range(2):
-            for first in (2, 0):
-                line = at_line(half_at, part, first, first + 2)
-                plan.arrive(("o2n", half_at, part, first), last_next.at[line], ahead[part])
-            for first in (0, 2):
-                line = at_line(half_at, part, first, first + 2)
-                plan.arrive(("o2p", half_at, part, first), last_prev.at[line], behind[part])
-            line = at_line(half_at, part)
             total = summed(at_block(half_at, part, 0))
-            total = total + last_next[line].astype(F32) + last_prev[line].astype(F32)
-            inner_out[line] = total.astype(BF16)
+            for at, to in reversed(outer_targets[part]):
+                line = at_line(half_at, part, at)
+                plan.arrive(("o", half_at, part, at), outer_in.at[line], to)
+                total = total + outer_in[line].astype(F32)
+            inner_out[at_line(half_at, part)] = total.astype(BF16)
             for at, to in inner_targets[part]:
                 block = (half_at, at, slice(None), columns[part])
                 plan.send(("i", half_at, part, at), inner_out.at[block], inner_in.at[block], to)
             half_sum[half_at, :, columns[part]] = total[0]
 
-    def inner_end(half_at):
-        for part in range(2):
-            total = half_sum[half_at, :, columns[part]]
-            for at, to in inner_targets[part]:
-                block = (half_at, at, slice(None), columns[part])
-                plan.arrive(("i", half_at, part, at), inner_in.at[block], to)
-                total = total + inner_in[block].astype(F32)
-            if half_at == 0:
-                half_out[:, columns[part]] = total.astype(BF16)
-            else:
-                half_sum[half_at, :, columns[part]] = total
-
+    def inner_end(half_at, part):
+        total = half_sum[half_at, :, columns[part]]
+        for at, to in reversed(inner_targets[part]):
+            block = (half_at, at, slice(None), columns[part])
+            plan.arrive(("i", half_at, part, at), inner_in.at[block], to)
+            total = total + inner_in[block].astype(F32)
+        if half_at == 0:
+            half_out[:, columns[part]] = total.astype(BF16)
+        else:
+            half_sum[half_at, :, columns[part]] = total
+
+    def give_token(at):
+        pl.semaphore_signal(token_sems.at[at], inc=1, device_id=token_target, device_id_type=MESH)
+
+    def take_token(at):
+        pl.semaphore_wait(token_sems.at[at], 1)
+
+    token_target = along_z[spread.lengths[-1]]
     last = len(spread.levels) - 1
+    cut = min(spread.slots[way, at] for way, at in spread.order if at in spread.levels[last])
+    early, late = (0, cut), (cut, blocks)
+    for level in range(last):
+        text_level(level)
+        if level < HALVES:
+            image_near(level)
+    for level in range(last, HALVES):
+        image_near(level)
+    image_far()
+    from_sibling(X_PREV, X_NEXT)
+    batch(early, X_OWN, X_FAR)
+    text_level(last)
+    give_token(0)
+    from_sibling(X_FAR)
+    batch(late, X_OWN, X_FAR + 1)
     back(last)
+    batch(early, X_FAR, X_FAR + 1)
+
     image_partial(0)
     image_partial(1)
+    take_token(0)
+    give_token(1)
     outer_start(0)
     for level in range(last - 1, 0, -1):
         back(level)
-    outer_second(0)
-    outer_start(1)
+    inner_start(0)
     if last > 0:
         back(0)
-    inner_start(0)
-    outer_second(1)
+    inner_end(0, 0)
+    inner_end(0, 1)
+    take_token(1)
+    plan.send(("h",), half_out, half_in, z_far)
+    outer_start(1)
 
     total = partial[0]
     for way in range(2):
         for child in spread.children(way, 0):
             total = total + back_arrival(way, child)
-    inner_end(0)
-    plan.send(("h",), half_out, half_in, z_far)
     unit_text, text_scaling = unit_rows(text_raw[...])
     grad_text_ref[...] = unit_backward(unit_text, text_scaling, scale * total)
 
     inner_start(1)
-    inner_end(1)
+    inner_end(1, 0)
+    inner_end(1, 1)
     own_row = pl.multiple_of(((y * HALVES + z_half) * CORES + core) * rows, rows)
     unit_image, image_scaling = unit_rows(image_raw[pl.ds(own_row, rows), :])
     plan.arrive(("h",), half_in, z_far)
@@ -454,16 +433,14 @@
             scratch(HALVES, RING, RING),
             scratch(HALVES, RING, RING, dtype=F32),
             scratch(HALVES, RING, RING),
-            scratch(HALVES, 2),
-            scratch(HALVES, 2),
-            scratch(HALVES, RING),
-            scratch(HALVES, RING),
+            scratch(HALVES, RING, RING),
             scratch(HALVES, RING),
             scratch(HALVES, RING),
             scratch(HALVES, dtype=F32),
             scratch(),
             scratch(),
             pltpu.SemaphoreType.DMA((2,)),
+            pltpu.SemaphoreType.REGULAR((2,)),
             pltpu.SemaphoreType.DMA((MOST_COPIES,)),
             pltpu.SemaphoreType.DMA((MOST_COPIES,)),
         ],

time: 73.7 us -> 71.2 us (0.966)
  the two profiles are of different devices: /device:TPU:6 before, /device:TPU:4 now
where the time goes in v3:
time: 71.2 us; the launch traced here: 71 us
  Pallas kernels  66.8 us (94%)
  local copies, waits for them, and re-layouts  2.19 us (3%)
  between operations  1.94 us (3%)
    pallas_call x1, Pallas kernels, per_device(): pl.pallas_call(functools.partial(kernel, zlo_size), out_shape=[jax.ShapeD...  66.8 us
    unnamed x4, local copies, waits for them, and re-layouts  2.19 us

profile of v3, /device:TPU:4, one launch (start us, length us, event | category | flops | bytes accessed | tf_op | source)
XLA Modules:
  0.0 71.0 jit_solution(10326585630332877438)
XLA Ops:
  1.9 66.8 %shard_map.59 = (f32[16,1152]{1,0:T(8,128)}, f32[16,1152]{1,0:T(8,128)}) custom-call(f32[1,1]{1,0:T(1,128)} %bitcast.2.scale_ref, f32[1,1]{1,0:T(1,128)} %bitcast.3.bias_ref, bf16[256,1152]{1,0:T(8,128)(2,1)} %image_hbm.1, bf16[16,1152]{1,0:T(8,128)(2,1)} %text_hbm.1), custom_call_target="tpu_custom_call" | custom-call | tf_op jit(solution)/shard_map/pallas_call | solution.py:418
  68.8 0.0 copy-start
  68.8 1.6 %copy.10 = f32[16,1152]{1,0:T(8,128)} copy(f32[16,1152]{1,0:T(8,128)} %get-tuple-element.4) | data formatting | bytes 147456
  70.3 0.0 copy-done
  70.3 0.6 copy.11
Async XLA Ops:
  68.8 1.6 %copy-start = (f32[16,1152]{1,0:T(8,128)S(1)}, f32[16,1152]{1,0:T(8,128)}, u32[]{:S(2)}) copy-start(f32[16,1152]{1,0:T(8,128)} %get-tuple-element.5) | copy-start | bytes 221188

commit v4 on v3

--- a/solution.py
+++ b/solution.py
@@ -266,7 +266,7 @@
             partial[slots[0] : slots[1]] += grads
 
     def back(level):
-        for at in reversed(spread.levels[level]):
+        for at in spread.levels[level]:
             for way in range(2):
                 if at <= spread.reach[way]:
                     slot = spread.slots[way, at]

time: 71.2 us -> 69.7 us (0.979)
  the two profiles are of different devices: /device:TPU:4 before, /device:TPU:6 now
where the time goes in v4:
time: 69.7 us; the launch traced here: 68.5 us
  Pallas kernels  64.4 us (92%)
  local copies, waits for them, and re-layouts  2.19 us (3%)
  between operations  1.94 us (3%)
    pallas_call x1, Pallas kernels, per_device(): pl.pallas_call(functools.partial(kernel, zlo_size), out_shape=[jax.ShapeD...  64.4 us
    unnamed x4, local copies, waits for them, and re-layouts  2.19 us

profile of v4, /device:TPU:6, one launch (start us, length us, event | category | flops | bytes accessed | tf_op | source)
XLA Modules:
  0.0 68.5 jit_solution(12533831182210684039)
XLA Ops:
  1.9 64.4 %shard_map.59 = (f32[16,1152]{1,0:T(8,128)}, f32[16,1152]{1,0:T(8,128)}) custom-call(f32[1,1]{1,0:T(1,128)} %bitcast.2.scale_ref, f32[1,1]{1,0:T(1,128)} %bitcast.3.bias_ref, bf16[256,1152]{1,0:T(8,128)(2,1)} %image_hbm.1, bf16[16,1152]{1,0:T(8,128)(2,1)} %text_hbm.1), custom_call_target="tpu_custom_call" | custom-call | tf_op jit(solution)/shard_map/pallas_call | solution.py:418
  66.3 0.0 copy-start
  66.3 1.6 %copy.10 = f32[16,1152]{1,0:T(8,128)} copy(f32[16,1152]{1,0:T(8,128)} %get-tuple-element.4) | data formatting | bytes 147456
  67.9 0.0 copy-done
  67.9 0.6 copy.11
Async XLA Ops:
  66.3 1.6 %copy-start = (f32[16,1152]{1,0:T(8,128)S(1)}, f32[16,1152]{1,0:T(8,128)}, u32[]{:S(2)}) copy-start(f32[16,1152]{1,0:T(8,128)} %get-tuple-element.5) | copy-start | bytes 221188

commit v5 on v4

--- a/solution.py
+++ b/solution.py
@@ -372,9 +372,9 @@
 
     image_partial(0)
     image_partial(1)
+    outer_start(0)
     take_token(0)
     give_token(1)
-    outer_start(0)
     for level in range(last - 1, 0, -1):
         back(level)
     inner_start(0)
@@ -386,6 +386,7 @@
     plan.send(("h",), half_out, half_in, z_far)
     outer_start(1)
 
+    inner_start(1)
     total = partial[0]
     for way in range(2):
         for child in spread.children(way, 0):
@@ -393,7 +394,6 @@
     unit_text, text_scaling = unit_rows(text_raw[...])
     grad_text_ref[...] = unit_backward(unit_text, text_scaling, scale * total)
 
-    inner_start(1)
     inner_end(1, 0)
     inner_end(1, 1)
     own_row = pl.multiple_of(((y * HALVES + z_half) * CORES + core) * rows, rows)

time: 69.7 us -> 69.7 us (level)
  no operation moved by 1% of the time
where the time goes in v5:
time: 69.7 us; the launch traced here: 68.5 us
  Pallas kernels  64.4 us (92%)
  local copies, waits for them, and re-layouts  2.19 us (3%)
  between operations  1.94 us (3%)
    pallas_call x1, Pallas kernels, per_device(): pl.pallas_call(functools.partial(kernel, zlo_size), out_shape=[jax.ShapeD...  64.4 us
    unnamed x4, local copies, waits for them, and re-layouts  2.19 us

profile of v5, /device:TPU:6, one launch (start us, length us, event | category | flops | bytes accessed | tf_op | source)
XLA Modules:
  0.0 68.5 jit_solution(67426411419120774)
XLA Ops:
  1.9 64.4 %shard_map.59 = (f32[16,1152]{1,0:T(8,128)}, f32[16,1152]{1,0:T(8,128)}) custom-call(f32[1,1]{1,0:T(1,128)} %bitcast.2.scale_ref, f32[1,1]{1,0:T(1,128)} %bitcast.3.bias_ref, bf16[256,1152]{1,0:T(8,128)(2,1)} %image_hbm.1, bf16[16,1152]{1,0:T(8,128)(2,1)} %text_hbm.1), custom_call_target="tpu_custom_call" | custom-call | tf_op jit(solution)/shard_map/pallas_call | solution.py:418
  66.3 0.0 copy-start
  66.3 1.6 %copy.10 = f32[16,1152]{1,0:T(8,128)} copy(f32[16,1152]{1,0:T(8,128)} %get-tuple-element.4) | data formatting | bytes 147456
  67.9 0.0 copy-done
  67.9 0.6 copy.11
Async XLA Ops:
  66.3 1.6 %copy-start = (f32[16,1152]{1,0:T(8,128)S(1)}, f32[16,1152]{1,0:T(8,128)}, u32[]{:S(2)}) copy-start(f32[16,1152]{1,0:T(8,128)} %get-tuple-element.5) | copy-start | bytes 221188
